TPU v7x, 256 devices: a whole 4x4x8 slice. The times are simulated.
256 devices in a mesh: grp: 32 (over z_lo, x, core), tp: 8 (over y, z_hi).
Axes of the slice: x: 4, y: 4, z: 8 (z_hi: 2, z_lo: 4; z = z_hi * 4 + z_lo), core: 2. Of those that a mesh axis runs over, the one named last changes fastest.
Arguments:
- q_attn: bfloat16 [64, 64, 4096], P('grp', None, 'tp'), may hold values from -6 to 6
- q_resid: bfloat16 [64, 64, 4096], P('grp', None, 'tp'), may hold values from -6 to 6
- p_attn: bfloat16 [64, 128, 4096], P('grp', None, 'tp'), may hold values from -6 to 6
- p_resid: bfloat16 [64, 128, 4096], P('grp', None, 'tp'), may hold values from -6 to 6
- w_out: bfloat16 [4096, 4096], P('grp', 'tp'), may hold values from -0.09375 to 0.09375
- w_snap: bfloat16 [4096, 4096], P('grp', 'tp'), may hold values from -0.09375 to 0.09375
- norm_gain: bfloat16 [4096], P('tp'), may hold values from 0.25 to 4
- pass_attn: bfloat16 [64, 256, 4096], P('grp', None, 'tp'), may hold values from -6 to 6
- pass_resid: bfloat16 [64, 256, 4096], P('grp', None, 'tp'), may hold values from -6 to 6
- pass_len: int32 [64], P('grp'), may hold values from 128 to 256, as said below
- block_owner: int32 [32], replicated, may hold values from 0 to 31, each once
- neg_ids: int32 [64, 8], P('grp'), may hold values from 0 to 63
Outputs:
- loss: float32 [], replicated
- w_grad: float32 [4096, 4096], P('grp', 'tp')
- passage_index: bfloat16 [64, 4096], P('grp', 'tp')
Inputs may be any that keep to these rules, and one draw needn't show every extreme that they name: `pass_len`: lengths are multiples of 128; in every block of 2 slots one passage has 256 tokens.
All inputs are finite; a program needn't handle non-finite values.
Results may differ from a plain program's by a relative error of at most 0.0034.
Values may be sent and summed in bfloat16 or wider, within the bound.
A program may use at most 64 MiB of HBM per device.

v0:
```python
import jax
import jax.numpy as jnp
from jax import lax
from jax.sharding import PartitionSpec as P

EPS = 1e-06
TEMP = 0.05


def add_block(tokens, piece):
    return jnp.dot(tokens, piece, preferred_element_type=jnp.float32)


def token_norm(hidden, squares, width, gain):
    factor = lax.rsqrt(squares[:, None] / width + EPS)
    return (factor, hidden * factor * gain[None, :])


def contract_rows(left, right):
    return lax.dot_general(
        left, right, (((0,), (0,)), ((), ())), preferred_element_type=jnp.float32
    )


def spread_tokens(values, count):
    seqs, cols = values.shape
    return jnp.broadcast_to(values[:, None, :], (seqs, count, cols)).reshape(seqs * count, cols)


def shards(
    q_attn,
    q_resid,
    p_attn,
    p_resid,
    w_out,
    w_snap,
    norm_gain,
    pass_attn,
    pass_resid,
    pass_len,
    block_owner,
    neg_ids,
):
    precise = lax.Precision.HIGHEST
    grp_size = lax.axis_size("grp")
    queries, qlen, cols = q_attn.shape
    width = cols * lax.axis_size("tp")
    poslen = p_attn.shape[1]
    blocks, plen = (pass_attn.shape[0], pass_attn.shape[1])
    gain = norm_gain.astype(jnp.float32)
    pass_full = lax.all_gather(pass_attn, "tp", axis=2, tiled=True).reshape(blocks * plen, width)
    query_full, pos_full = (
        lax.all_gather(q_attn, "tp", axis=2, tiled=True),
        lax.all_gather(p_attn, "tp", axis=2, tiled=True),
    )
    query_full = query_full.reshape(queries * qlen, width)
    pos_full = pos_full.reshape(queries * poslen, width)
    proj_s = add_block(pass_full, lax.all_gather(w_snap, "grp", axis=0, tiled=True))
    piece = lax.all_gather(w_out, "grp", axis=0, tiled=True)
    proj_q = add_block(query_full, piece)
    proj_p = add_block(pos_full, piece)
    hidden_s = pass_resid.reshape(blocks * plen, cols).astype(jnp.float32) + proj_s
    squares_s = lax.psum(jnp.sum(hidden_s * hidden_s, axis=1), "tp")
    factor_s, out_s = token_norm(hidden_s, squares_s, width, gain)
    mask = (lax.broadcasted_iota(jnp.int32, (blocks, plen), 1) < pass_len[:, None]).astype(
        jnp.float32
    )
    pooled_s = jnp.sum(out_s.reshape(blocks, plen, cols) * mask[:, :, None], axis=1) / pass_len[
        :, None
    ].astype(jnp.float32)
    pool_sq = lax.psum(jnp.sum(pooled_s * pooled_s, axis=1), "tp")
    passage_index = (pooled_s * lax.rsqrt(pool_sq[:, None] / width + EPS)).astype(jnp.bfloat16)
    hidden_q = q_resid.reshape(queries * qlen, cols).astype(jnp.float32) + proj_q
    hidden_p = p_resid.reshape(queries * poslen, cols).astype(jnp.float32) + proj_p
    squares_q, squares_p = lax.psum(
        (jnp.sum(hidden_q * hidden_q, axis=1), jnp.sum(hidden_p * hidden_p, axis=1)), "tp"
    )
    factor_q, out_q = token_norm(hidden_q, squares_q, width, gain)
    factor_p, out_p = token_norm(hidden_p, squares_p, width, gain)
    pooled_q = jnp.mean(out_q.reshape(queries, qlen, cols), axis=1)
    pooled_p = jnp.mean(out_p.reshape(queries, poslen, cols), axis=1)
    index_all = lax.all_gather(passage_index, "grp", axis=0, tiled=True)
    owners = block_owner.shape[0]
    match = (neg_ids // blocks)[:, :, None] == lax.broadcasted_iota(jnp.int32, (1, 1, owners), 2)
    owner_of = jnp.sum(jnp.where(match, block_owner[None, None, :], 0), axis=2)
    slots = owner_of * blocks + neg_ids % blocks
    neg_rows = index_all[slots].astype(jnp.float32)
    sq_q, sq_p = lax.psum(
        (jnp.sum(pooled_q * pooled_q, axis=1), jnp.sum(pooled_p * pooled_p, axis=1)), "tp"
    )
    norm_q = lax.rsqrt(sq_q / width + EPS)
    norm_p = lax.rsqrt(sq_p / width + EPS)
    emb_q = pooled_q * norm_q[:, None]
    emb_p = pooled_p * norm_p[:, None]
    pos, neg = lax.psum(
        (
            jnp.sum(emb_q * emb_p, axis=1),
            jnp.einsum("qc,qjc->qj", emb_q, neg_rows, precision=precise),
        ),
        "tp",
    )
    scale = 1.0 / (width * TEMP)
    exp_pos = jnp.exp(pos * scale)
    exp_neg = jnp.exp(neg * scale)
    total = exp_pos + jnp.sum(exp_neg, axis=1)
    terms = jnp.log(total) - pos * scale
    loss = lax.psum(jnp.sum(terms), "grp") / (queries * grp_size)
    d_pos = exp_pos / total - 1.0
    d_neg = exp_neg / total[:, None]
    grad_q = (
        d_pos[:, None] * emb_p + jnp.einsum("qj,qjc->qc", d_neg, neg_rows, precision=precise)
    ) * scale
    grad_p = d_pos[:, None] * emb_q * scale
    back_q, back_p = lax.psum(
        (jnp.sum(emb_q * grad_q, axis=1), jnp.sum(emb_p * grad_p, axis=1)), "tp"
    )
    seq_q = norm_q[:, None] * (grad_q - emb_q * back_q[:, None] / width)
    seq_p = norm_p[:, None] * (grad_p - emb_p * back_p[:, None] / width)
    upper_q = spread_tokens(seq_q / qlen * gain[None, :], qlen)
    upper_p = spread_tokens(seq_p / poslen * gain[None, :], poslen)
    normed_q = hidden_q * factor_q
    normed_p = hidden_p * factor_p
    inner_q, inner_p = lax.psum(
        (jnp.sum(normed_q * upper_q, axis=1), jnp.sum(normed_p * upper_p, axis=1)), "tp"
    )
    dh_q = (factor_q * (upper_q - normed_q * inner_q[:, None] / width)).astype(jnp.bfloat16)
    dh_p = (factor_p * (upper_p - normed_p * inner_p[:, None] / width)).astype(jnp.bfloat16)
    w_grad = lax.psum_scatter(
        contract_rows(query_full, dh_q) + contract_rows(pos_full, dh_p),
        "grp",
        scatter_dimension=0,
        tiled=True,
    )
    return (loss, w_grad, passage_index)


def solution(mesh):
    placed = (
        P("grp", None, "tp"),
        P("grp", None, "tp"),
        P("grp", None, "tp"),
        P("grp", None, "tp"),
        P("grp", "tp"),
        P("grp", "tp"),
        P("tp"),
        P("grp", None, "tp"),
        P("grp", None, "tp"),
        P("grp"),
        P(),
        P("grp", None),
    )
    return jax.shard_map(
        shards,
        mesh=mesh,
        in_specs=placed,
        out_specs=(P(), P("grp", "tp"), P("grp", "tp")),
        check_vma=False,
    )
```

profile of v0, /device:TPU:24, one launch (start us, length us, event | category | flops | bytes accessed | tf_op | source)
XLA Modules:
  0.0 736.5 jit_solution(12068333558267169497)
XLA Ops:
  7.2 0.0 all-gather.7.cloned.1.call-start
  7.2 0.7 all-gather.7.cloned.1.call-update
  7.9 0.0 all-gather.9.cloned.1.call-start
  8.0 0.7 all-gather.9.cloned.1.call-update
  8.7 0.0 all-gather.11.cloned.1.call-start
  8.7 0.7 all-gather.11.cloned.1.call-update
  9.4 0.0 all-gather.13.cloned.1.call-start
  9.4 0.5 all-gather.13.cloned.1.call-update
  10.0 0.0 all-gather.15.cloned.1.call-start
  10.0 0.5 all-gather.15.cloned.1.call-update
  10.6 0.0 reduce-scatter.2.cloned.1.call-start
  10.6 0.7 convert_element_type.44
  11.3 0.7 convert_element_type.50
  11.9 0.7 and_select_fusion.1
  12.6 0.9 select_reduce_fusion
  13.5 0.7 compare_select_fusion
  14.2 0.1 reshape.170
  14.3 0.7 compare_convert_fusion
  15.0 0.7 broadcast_multiply_fusion.2
  15.7 58.9 %all-gather.7.cloned.1.call-done = bf16[2,64,4096]{2,1,0:T(8,128)(2,1)} async-done(((bf16[2,64,512]{2,1,0:T(8,128)(2,1)}), bf16[2,64,4096]{2,1,0:T(8,128)(2,1)}) %all-gather.7.cloned.1.call-update) | async-done | bytes 1048592 | tf_op jit(solution)/shard_map/all_gather | solution.py:53
  74.6 60.8 %all-gather.9.cloned.1.call-done = bf16[4096,512]{1,0:T(8,128)(2,1)} async-done(((bf16[128,512]{1,0:T(8,128)(2,1)}), bf16[4096,512]{1,0:T(8,128)(2,1)}) %all-gather.9.cloned.1.call-update) | async-done | bytes 4194320 | tf_op jit(solution)/shard_map/all_gather | solution.py:59
  135.4 3.3 multiply_reduce_fusion.3
  138.7 0.0 copy-start.2
  138.7 74.5 %all-gather.11.cloned.1.call-done = bf16[2,128,4096]{2,1,0:T(8,128)(2,1)} async-done(((bf16[2,128,512]{2,1,0:T(8,128)(2,1)}), bf16[2,128,4096]{2,1,0:T(8,128)(2,1)}) %all-gather.11.cloned.1.call-update) | async-done | bytes 2097168 | tf_op jit(solution)/shard_map/all_gather | solution.py:54
  213.2 4.2 multiply_reduce_fusion.2
  217.3 105.9 %all-gather.13.cloned.1.call-done = bf16[2,256,4096]{2,1,0:T(8,128)(2,1)} async-done(((bf16[2,256,512]{2,1,0:T(8,128)(2,1)}), bf16[2,256,4096]{2,1,0:T(8,128)(2,1)}) %all-gather.13.cloned.1.call-update) | async-done | bytes 4194320 | tf_op jit(solution)/shard_map/all_gather | solution.py:51
  323.2 60.6 %all-gather.15.cloned.1.call-done = bf16[4096,512]{1,0:T(8,128)(2,1)} async-done(((bf16[128,512]{1,0:T(8,128)(2,1)}), bf16[4096,512]{1,0:T(8,128)(2,1)}) %all-gather.15.cloned.1.call-update) | async-done | bytes 4194320 | tf_op jit(solution)/shard_map/all_gather | solution.py:58
  383.9 5.9 multiply_reduce_fusion.1
  389.8 27.1 %all-reduce.4 = (f32[256]{0:T(256)S(1)}, f32[128]{0:T(128)S(1)}, f32[512]{0:T(512)S(1)}) all-reduce(f32[256]{0:T(256)S(1)} %get-tuple-element.42, f32[128]{0:T(128)S(1)} %get-tuple-element.44, f32[512]{0:T(512)S(1)} %get-tuple-element.46), channel_id=1, replica_groups=mesh['grp'=32,'tp'=8] {'tp'}, use_global_device_ids=true, to_apply=%region_6.0 | all-reduce | flops 896 | bytes 7168 | tf_op jit(solution)/shard_map/psum | solution.py:75
  416.9 0.1 bitcast_reduce_fusion
  417.0 0.1 multiply_reduce_fusion.8
  417.1 0.1 bitcast_reduce_fusion.1
  417.3 0.1 multiply_reduce_fusion.9
  417.4 0.2 multiply_reduce_fusion
  417.6 0.2 multiply_reduce_fusion.6
  417.8 24.8 %all-reduce.3 = (f32[2]{0:T(128)S(1)}, f32[2]{0:T(128)S(1)}, f32[2]{0:T(128)S(1)}) all-reduce(f32[2]{0:T(128)S(1)} %multiply_reduce_fusion.8, f32[2]{0:T(128)S(1)} %multiply_reduce_fusion.9, f32[2]{0:T(128)S(1)} %get-tuple-element.27), channel_id=1, replica_groups=mesh['grp'=32,'tp'=8] {'tp'}, use_global_device_ids=true, to_apply=%region_9.0 | all-reduce | flops 6 | bytes 48 | tf_op jit(solution)/shard_map/psum | solution.py:88
  442.6 0.1 fusion.29
  442.7 40.8 %all-gather = bf16[32,2,512]{2,1,0:T(2,128)(2,1)S(1)} all-gather(bf16[1,2,512]{2,1,0:T(2,128)(2,1)S(1)} %fusion.29), channel_id=1, replica_groups=mesh['grp'=32,'tp'=8] {'grp'}, dimensions={0}, use_global_device_ids=true | all-gather | bytes 67584 | tf_op jit(solution)/shard_map/all_gather | solution.py:82
  483.5 0.6 gather_fusion
  484.1 0.2 fusion.15
  484.3 0.1 fusion.6
  484.4 28.9 %all-reduce.2 = (f32[2]{0:T(128)S(1)}, f32[2,8]{1,0:T(2,128)S(1)}) all-reduce(f32[2]{0:T(128)S(1)} %get-tuple-element.32, f32[2,8]{1,0:T(2,128)S(1)} %bitcast.74), channel_id=1, replica_groups=mesh['grp'=32,'tp'=8] {'tp'}, use_global_device_ids=true, to_apply=%region_11.12 | all-reduce | flops 18 | bytes 144 | tf_op jit(solution)/shard_map/psum | solution.py:95
  513.2 0.1 fusion.14
  513.4 0.6 exponential_add_fusion
  514.0 0.1 fusion.13
  514.1 0.1 fusion.8
  514.2 0.2 multiply_reduce_fusion.4
  514.4 24.8 %all-reduce.1 = (f32[2]{0:T(128)S(1)}, f32[2]{0:T(128)S(1)}) all-reduce(f32[2]{0:T(128)S(1)} %get-tuple-element.13, f32[2]{0:T(128)S(1)} %get-tuple-element.12), channel_id=1, replica_groups=mesh['grp'=32,'tp'=8] {'tp'}, use_global_device_ids=true, to_apply=%region_23.24 | all-reduce | flops 4 | bytes 32 | tf_op jit(solution)/shard_map/psum | solution.py:114
  539.2 0.1 multiply_multiply_fusion.3
  539.2 0.2 fusion
  539.4 0.2 fusion.3
  539.6 28.9 %all-reduce = (f32[128]{0:T(128)S(1)}, f32[256]{0:T(256)S(1)}) all-reduce(f32[128]{0:T(128)S(1)} %fusion.3, f32[256]{0:T(256)S(1)} %fusion), channel_id=1, replica_groups=mesh['grp'=32,'tp'=8] {'tp'}, use_global_device_ids=true, to_apply=%region_25.26 | all-reduce | flops 384 | bytes 3072 | tf_op jit(solution)/shard_map/psum | solution.py:123
  568.5 0.1 fusion.5
  568.6 0.0 copy-done
  568.6 0.0 copy-start.1
  568.6 1.3 fusion.17
  569.9 0.2 fusion.2
  570.1 0.1 copy-done.1
  570.2 4.5 add_bitcast_fusion
  574.8 0.0 reduce-scatter.2.cloned.1.call-update
  574.8 68.1 %psum.99 = f32[]{:T(128)} all-reduce(f32[]{:T(128)} %get-tuple-element.36), channel_id=1, replica_groups=mesh['grp'=32,'tp'=8] {'grp'}, use_global_device_ids=true, to_apply=%region_21.22 | all-reduce | flops 1 | bytes 8 | tf_op jit(solution)/shard_map/psum | solution.py:107
  643.5 0.7 multiply_convert_fusion
  644.2 82.5 %reduce-scatter.2.cloned.1.call-done = f32[128,512]{0,1:T(8,128)} async-done(((f32[4096,512]{0,1:T(8,128)}), f32[128,512]{0,1:T(8,128)}) %reduce-scatter.2.cloned.1.call-update) | async-done | bytes 262160 | tf_op jit(solution)/shard_map/reduce_scatter | solution.py:128
  726.7 1.8 copy.17
  (11 shorter events, 0.1 us)
Async XLA Ops:
  7.2 206.0 %copy-start.3 = (bf16[2,128,512]{2,1,0:T(8,128)(2,1)S(1)}, bf16[2,128,512]{2,1,0:T(8,128)(2,1)}, u32[]{:S(2)}) copy-start(bf16[2,128,512]{2,1,0:T(8,128)(2,1)} %param.15) | copy-start | bytes 786436
  7.2 67.4 %all-gather.7.cloned.1.call-start = ((), (), s32[]{:S(2)}) async-start(), calls=%async_computation.1 | async-start | bytes 1179648 | tf_op jit(solution)/shard_map/all_gather | solution.py:53
  7.9 127.5 %all-gather.9.cloned.1.call-start = ((), (), s32[]{:S(2)}) async-start(), calls=%async_computation.2 | async-start | bytes 4325376 | tf_op jit(solution)/shard_map/all_gather | solution.py:59
  8.7 204.5 %all-gather.11.cloned.1.call-start = ((), (), s32[]{:S(2)}) async-start(), calls=%async_computation.3 | async-start | bytes 2359296 | tf_op jit(solution)/shard_map/all_gather | solution.py:54
  9.4 313.8 %all-gather.13.cloned.1.call-start = ((), (), s32[]{:S(2)}) async-start(), calls=%async_computation.4 | async-start | bytes 4718592 | tf_op jit(solution)/shard_map/all_gather | solution.py:51
  10.0 373.9 %all-gather.15.cloned.1.call-start = ((), (), s32[]{:S(2)}) async-start(), calls=%async_computation.5 | async-start | bytes 4325376 | tf_op jit(solution)/shard_map/all_gather | solution.py:58
  10.6 716.1 %reduce-scatter.2.cloned.1.call-start = ((), (), s32[]{:S(2)}) async-start(), calls=%async_computation.6 | async-start | bytes 8650752 | tf_op jit(solution)/shard_map/reduce_scatter | solution.py:128
  138.7 245.2 %copy-start.2 = (bf16[2,256,512]{2,1,0:T(8,128)(2,1)S(1)}, bf16[2,256,512]{2,1,0:T(8,128)(2,1)}, u32[]{:S(2)}) copy-start(bf16[2,256,512]{2,1,0:T(8,128)(2,1)} %param.20) | copy-start | bytes 1572868
  389.7 178.9 %copy-start = (bf16[2,64,4096]{2,1,0:T(8,128)(2,1)S(1)}, bf16[2,64,4096]{2,1,0:T(8,128)(2,1)}, u32[]{:S(2)}) copy-start(bf16[2,64,4096]{2,1,0:T(8,128)(2,1)} %all-gather.7.cloned.1.call-done) | copy-start | bytes 3145732
  568.6 1.6 copy-start.1
Sparse Core Ops, SparseCore 0:
  10.5 64.0 all-gather.6
  76.5 58.8 all-gather.8
  137.9 75.2 all-gather.10
  215.5 107.6 all-gather.12
  324.9 58.8 all-gather.14
  574.9 151.7 reduce-scatter.1
where the time goes:
time: 737 us; the launch traced here: 736 us
  waiting for transfers between devices  446 us (61%)
  blocking collectives  243 us (33%)
  matrix products  19.4 us (3%)
  between operations  16 us (2%)
  other arithmetic  8.61 us (1%)
    all_gather x1, waiting for transfers between devices, shards(): lax.all_gather(pass_attn, 'tp', axis=2, tiled=True)  106 us
    reduce_scatter x1, waiting for transfers between devices, shards(): lax.psum_scatter(contract_rows(query_full, dh_q) + contract_rows(pos_full...  82.5 us
    all_gather x1, waiting for transfers between devices, shards(): lax.all_gather(p_attn, 'tp', axis=2, tiled=True)  74.5 us
    psum x1, blocking collectives, shards(): loss = lax.psum(jnp.sum(terms), 'grp') / (queries * grp_size)  68.1 us
    all_gather x1, waiting for transfers between devices, shards(): piece = lax.all_gather(w_out, 'grp', axis=0, tiled=True)  60.8 us
    all_gather x1, waiting for transfers between devices, shards(): lax.all_gather(w_snap, 'grp', axis=0, tiled=True)  60.6 us
    all_gather x1, waiting for transfers between devices, shards(): lax.all_gather(q_attn, 'tp', axis=2, tiled=True)  58.9 us
    all_gather x1, blocking collectives, shards(): index_all = lax.all_gather(passage_index, 'grp', axis=0, tiled=True)  40.8 us
  transfers between devices with their start and end apart: 6, of which 6 were waited for; matrix products, arithmetic and copies ran while one was open for 2% of the time, Pallas kernels for 0%

commit v1 on v0

--- a/solution.py
+++ b/solution.py
@@ -55,7 +55,12 @@
     )
     query_full = query_full.reshape(queries * qlen, width)
     pos_full = pos_full.reshape(queries * poslen, width)
-    proj_s = add_block(pass_full, lax.all_gather(w_snap, "grp", axis=0, tiled=True))
+    proj_s = add_block(
+        pass_full,
+        jnp.concatenate(
+            lax.all_to_all(jnp.stack([w_snap] * lax.axis_size("grp")), "grp", 0, 0), axis=0
+        ),
+    )
     piece = lax.all_gather(w_out, "grp", axis=0, tiled=True)
     proj_q = add_block(query_full, piece)
     proj_p = add_block(pos_full, piece)

time: 737 us -> 704 us (0.955)
  waiting for transfers between devices: 446 us -> 408 us
  starting transfers between devices: 0.23 us -> 9.22 us
    all_gather x1 -> x0, waiting for transfers between devices: 60.6 us -> none  [shards(): lax.all_gather(w_snap, 'grp', axis=0, tiled=True)]
    all_gather x1, waiting for transfers between devices: 60.8 us -> 79 us  [shards(): piece = lax.all_gather(w_out, 'grp', axis=0, tiled=True)]
    all_to_all x0 -> x1, starting transfers between devices: none -> 9.02 us  [shards(): lax.all_to_all(jnp.stack([w_snap] * lax.axis_size('grp')), 'grp', 0, 0)]
  transfers between devices with their start and end apart: 6 -> 6, of which waited for: 6 -> 5; matrix products, arithmetic and copies ran while one was open for 2% -> 2% of each run, Pallas kernels for 0% -> 0%
where the time goes in v1:
time: 704 us; the launch traced here: 703 us
  waiting for transfers between devices  408 us (58%)
  blocking collectives  241 us (34%)
  matrix products  19.5 us (3%)
  between operations  15.7 us (2%)
  starting transfers between devices  9.22 us (1%)
    all_gather x1, waiting for transfers between devices, shards(): lax.all_gather(pass_attn, 'tp', axis=2, tiled=True)  108 us
    reduce_scatter x1, waiting for transfers between devices, shards(): lax.psum_scatter(contract_rows(query_full, dh_q) + contract_rows(pos_full...  83.6 us
    all_gather x1, waiting for transfers between devices, shards(): lax.all_gather(p_attn, 'tp', axis=2, tiled=True)  80.8 us
    all_gather x1, waiting for transfers between devices, shards(): piece = lax.all_gather(w_out, 'grp', axis=0, tiled=True)  79 us
    psum x1, blocking collectives, shards(): loss = lax.psum(jnp.sum(terms), 'grp') / (queries * grp_size)  68 us
    all_gather x1, waiting for transfers between devices, shards(): lax.all_gather(q_attn, 'tp', axis=2, tiled=True)  53.8 us
    all_gather x1, blocking collectives, shards(): index_all = lax.all_gather(passage_index, 'grp', axis=0, tiled=True)  39.6 us
    psum x1, blocking collectives, shards(): lax.psum((jnp.sum(pooled_q * pooled_q, axis=1), jnp.sum(pooled_p * pooled...  28.9 us
  transfers between devices with their start and end apart: 6, of which 5 were waited for; matrix products, arithmetic and copies ran while one was open for 2% of the time, Pallas kernels for 0%

profile of v1, /device:TPU:24, one launch (start us, length us, event | category | flops | bytes accessed | tf_op | source)
XLA Modules:
  0.0 703.2 jit_solution(9942183420980986301)
XLA Ops:
  7.2 0.0 all-gather.10.cloned.1.call-start
  7.2 0.7 all-gather.10.cloned.1.call-update
  7.9 0.0 all-gather.8.cloned.1.call-start
  7.9 0.7 all-gather.8.cloned.1.call-update
  8.6 0.0 all-gather.12.cloned.1.call-start
  8.7 0.7 all-gather.12.cloned.1.call-update
  9.4 3.3 stack.2
  12.7 0.0 copy-start.8
  12.7 9.0 %all-to-all-start = ((bf16[32,128,512]{2,1,0:T(8,128)(2,1)}), bf16[32,128,512]{2,1,0:T(8,128)(2,1)}, u32[]{:S(2)}, u32[]{:S(2)}) async-start(bf16[32,128,512]{2,1,0:T(8,128)(2,1)} %stack.2), calls=%async_computation | async-start | bytes 8388608 | tf_op jit(solution)/shard_map/all_to_all | solution.py:61
  21.8 0.0 copy-start.7
  21.8 0.0 all-gather.6.cloned.1.call-start
  21.8 0.5 all-gather.6.cloned.1.call-update
  22.4 0.0 reduce-scatter.2.cloned.1.call-start
  22.4 0.0 copy-done.4
  22.4 0.0 copy-done.5
  22.4 0.2 select_reduce_fusion
  22.7 0.0 copy-done.3
  22.7 0.0 copy-done.6
  22.7 0.1 reshape.176
  22.8 0.1 compare_convert_fusion
  22.9 80.8 %all-gather.10.cloned.1.call-done = bf16[2,128,4096]{2,1,0:T(8,128)(2,1)} async-done(((bf16[2,128,512]{2,1,0:T(8,128)(2,1)}), bf16[2,128,4096]{2,1,0:T(8,128)(2,1)}) %all-gather.10.cloned.1.call-update) | async-done | bytes 2097168 | tf_op jit(solution)/shard_map/all_gather | solution.py:54
  103.7 79.0 %all-gather.8.cloned.1.call-done = bf16[4096,512]{1,0:T(8,128)(2,1)} async-done(((bf16[128,512]{1,0:T(8,128)(2,1)}), bf16[4096,512]{1,0:T(8,128)(2,1)}) %all-gather.8.cloned.1.call-update) | async-done | bytes 4194320 | tf_op jit(solution)/shard_map/all_gather | solution.py:64
  182.7 0.0 copy-done.8
  182.7 4.1 multiply_reduce_fusion.2
  186.9 108.1 %all-gather.12.cloned.1.call-done = bf16[2,256,4096]{2,1,0:T(8,128)(2,1)} async-done(((bf16[2,256,512]{2,1,0:T(8,128)(2,1)}), bf16[2,256,4096]{2,1,0:T(8,128)(2,1)}) %all-gather.12.cloned.1.call-update) | async-done | bytes 4194320 | tf_op jit(solution)/shard_map/all_gather | solution.py:51
  295.0 0.0 all-to-all-done
  295.0 0.0 copy-done.7
  295.0 5.9 multiply_reduce_fusion.1
  300.9 53.8 %all-gather.6.cloned.1.call-done = bf16[2,64,4096]{2,1,0:T(8,128)(2,1)} async-done(((bf16[2,64,512]{2,1,0:T(8,128)(2,1)}), bf16[2,64,4096]{2,1,0:T(8,128)(2,1)}) %all-gather.6.cloned.1.call-update) | async-done | bytes 1048592 | tf_op jit(solution)/shard_map/all_gather | solution.py:53
  354.7 3.4 multiply_reduce_fusion.3
  358.1 21.7 %all-reduce.4 = (f32[256]{0:T(256)S(1)}, f32[128]{0:T(128)S(1)}, f32[512]{0:T(512)S(1)}) all-reduce(f32[256]{0:T(256)S(1)} %get-tuple-element.42, f32[128]{0:T(128)S(1)} %get-tuple-element.44, f32[512]{0:T(512)S(1)} %get-tuple-element.46), channel_id=1, replica_groups=mesh['grp'=32,'tp'=8] {'tp'}, use_global_device_ids=true, to_apply=%region_6.0 | all-reduce | flops 896 | bytes 7168 | tf_op jit(solution)/shard_map/psum | solution.py:80
  379.9 0.1 bitcast_reduce_fusion
  380.0 0.1 multiply_reduce_fusion.8
  380.2 0.1 bitcast_reduce_fusion.1
  380.3 0.1 multiply_reduce_fusion.9
  380.4 0.2 multiply_reduce_fusion
  380.6 0.2 multiply_reduce_fusion.6
  380.8 28.9 %all-reduce.3 = (f32[2]{0:T(128)S(1)}, f32[2]{0:T(128)S(1)}, f32[2]{0:T(128)S(1)}) all-reduce(f32[2]{0:T(128)S(1)} %multiply_reduce_fusion.8, f32[2]{0:T(128)S(1)} %multiply_reduce_fusion.9, f32[2]{0:T(128)S(1)} %get-tuple-element.27), channel_id=1, replica_groups=mesh['grp'=32,'tp'=8] {'tp'}, use_global_device_ids=true, to_apply=%region_9.0 | all-reduce | flops 6 | bytes 48 | tf_op jit(solution)/shard_map/psum | solution.py:93
  409.7 0.1 fusion.29
  409.8 39.6 %all-gather = bf16[32,2,512]{2,1,0:T(2,128)(2,1)S(1)} all-gather(bf16[1,2,512]{2,1,0:T(2,128)(2,1)S(1)} %fusion.29), channel_id=1, replica_groups=mesh['grp'=32,'tp'=8] {'grp'}, dimensions={0}, use_global_device_ids=true | all-gather | bytes 67584 | tf_op jit(solution)/shard_map/all_gather | solution.py:87
  449.4 0.6 gather_fusion
  450.0 0.2 fusion.15
  450.2 0.1 fusion.6
  450.3 28.7 %all-reduce.2 = (f32[2]{0:T(128)S(1)}, f32[2,8]{1,0:T(2,128)S(1)}) all-reduce(f32[2]{0:T(128)S(1)} %get-tuple-element.32, f32[2,8]{1,0:T(2,128)S(1)} %bitcast.75), channel_id=1, replica_groups=mesh['grp'=32,'tp'=8] {'tp'}, use_global_device_ids=true, to_apply=%region_11.12 | all-reduce | flops 18 | bytes 144 | tf_op jit(solution)/shard_map/psum | solution.py:100
  479.0 0.1 fusion.14
  479.1 0.6 exponential_add_fusion
  479.8 0.1 fusion.13
  479.8 0.1 fusion.8
  480.0 0.2 multiply_reduce_fusion.4
  480.2 24.9 %all-reduce.1 = (f32[2]{0:T(128)S(1)}, f32[2]{0:T(128)S(1)}) all-reduce(f32[2]{0:T(128)S(1)} %get-tuple-element.13, f32[2]{0:T(128)S(1)} %get-tuple-element.12), channel_id=1, replica_groups=mesh['grp'=32,'tp'=8] {'tp'}, use_global_device_ids=true, to_apply=%region_23.24 | all-reduce | flops 4 | bytes 32 | tf_op jit(solution)/shard_map/psum | solution.py:119
  505.1 0.1 multiply_multiply_fusion.3
  505.2 0.2 fusion
  505.4 0.2 fusion.3
  505.6 28.7 %all-reduce = (f32[128]{0:T(128)S(1)}, f32[256]{0:T(256)S(1)}) all-reduce(f32[128]{0:T(128)S(1)} %fusion.3, f32[256]{0:T(256)S(1)} %fusion), channel_id=1, replica_groups=mesh['grp'=32,'tp'=8] {'tp'}, use_global_device_ids=true, to_apply=%region_25.26 | all-reduce | flops 384 | bytes 3072 | tf_op jit(solution)/shard_map/psum | solution.py:128
  534.3 0.2 fusion.2
  534.5 0.1 fusion.5
  534.6 1.3 fusion.17
  535.9 0.3 copy-done.1
  536.2 4.5 add_bitcast_fusion
  540.7 0.0 reduce-scatter.2.cloned.1.call-update
  540.8 68.0 %psum.99 = f32[]{:T(128)} all-reduce(f32[]{:T(128)} %get-tuple-element.36), channel_id=1, replica_groups=mesh['grp'=32,'tp'=8] {'grp'}, use_global_device_ids=true, to_apply=%region_21.22 | all-reduce | flops 1 | bytes 8 | tf_op jit(solution)/shard_map/psum | solution.py:112
  609.5 0.7 multiply_convert_fusion
  610.1 83.6 %reduce-scatter.2.cloned.1.call-done = f32[128,512]{0,1:T(8,128)} async-done(((f32[4096,512]{0,1:T(8,128)}), f32[128,512]{0,1:T(8,128)}) %reduce-scatter.2.cloned.1.call-update) | async-done | bytes 262160 | tf_op jit(solution)/shard_map/reduce_scatter | solution.py:133
  693.7 1.8 copy.17
  (21 shorter events, 0.1 us)
Async XLA Ops:
  7.2 96.5 %all-gather.10.cloned.1.call-start = ((), (), s32[]{:S(2)}) async-start(), calls=%async_computation.4 | async-start | bytes 2359296 | tf_op jit(solution)/shard_map/all_gather | solution.py:54
  7.9 174.8 %all-gather.8.cloned.1.call-start = ((), (), s32[]{:S(2)}) async-start(), calls=%async_computation.3 | async-start | bytes 4325376 | tf_op jit(solution)/shard_map/all_gather | solution.py:64
  8.6 286.3 %all-gather.12.cloned.1.call-start = ((), (), s32[]{:S(2)}) async-start(), calls=%async_computation.5 | async-start | bytes 4718592 | tf_op jit(solution)/shard_map/all_gather | solution.py:51
  12.7 9.7 %copy-start.4 = (s32[2,8]{1,0:T(2,128)S(1)}, s32[2,8]{1,0:T(2,128)}, u32[]{:S(2)}) copy-start(s32[2,8]{1,0:T(2,128)} %param.23) | copy-start | bytes 196
  12.7 9.7 %copy-start.5 = (s32[32]{0:T(128)S(1)}, s32[32]{0:T(128)}, u32[]{:S(2)}) copy-start(s32[32]{0:T(128)} %param.22) | copy-start | bytes 388
  12.7 10.0 %copy-start.3 = (bf16[512]{0:T(512)(128)(2,1)S(1)}, bf16[512]{0:T(512)(128)(2,1)}, u32[]{:S(2)}) copy-start(bf16[512]{0:T(512)(128)(2,1)} %param.18) | copy-start | bytes 3076
  12.7 10.0 %copy-start.6 = (s32[2]{0:T(128)S(1)}, s32[2]{0:T(128)}, u32[]{:S(2)}) copy-start(s32[2]{0:T(128)} %param.21) | copy-start | bytes 28
  12.7 170.0 %copy-start.8 = (bf16[2,128,512]{2,1,0:T(8,128)(2,1)S(1)}, bf16[2,128,512]{2,1,0:T(8,128)(2,1)}, u32[]{:S(2)}) copy-start(bf16[2,128,512]{2,1,0:T(8,128)(2,1)} %param.15) | copy-start | bytes 786436
  12.7 282.3 %all-to-all-start = ((bf16[32,128,512]{2,1,0:T(8,128)(2,1)}), bf16[32,128,512]{2,1,0:T(8,128)(2,1)}, u32[]{:S(2)}, u32[]{:S(2)}) async-start(bf16[32,128,512]{2,1,0:T(8,128)(2,1)} %stack.2), calls=%async_computation | async-start | bytes 8388608 | tf_op jit(solution)/shard_map/all_to_all | solution.py:61
  21.8 273.2 %copy-start.7 = (bf16[2,256,512]{2,1,0:T(8,128)(2,1)S(1)}, bf16[2,256,512]{2,1,0:T(8,128)(2,1)}, u32[]{:S(2)}) copy-start(bf16[2,256,512]{2,1,0:T(8,128)(2,1)} %param.20) | copy-start | bytes 1572868
  21.8 332.9 %all-gather.6.cloned.1.call-start = ((), (), s32[]{:S(2)}) async-start(), calls=%async_computation.2 | async-start | bytes 1179648 | tf_op jit(solution)/shard_map/all_gather | solution.py:53
  22.4 671.3 %reduce-scatter.2.cloned.1.call-start = ((), (), s32[]{:S(2)}) async-start(), calls=%async_computation.6 | async-start | bytes 8650752 | tf_op jit(solution)/shard_map/reduce_scatter | solution.py:133
  295.0 59.7 %copy-start.2 = (bf16[2,64,512]{2,1,0:T(8,128)(2,1)S(1)}, bf16[2,64,512]{2,1,0:T(8,128)(2,1)}, u32[]{:S(2)}) copy-start(bf16[2,64,512]{2,1,0:T(8,128)(2,1)} %param.13) | copy-start | bytes 393220
  354.7 179.9 %copy-start = (bf16[2,64,4096]{2,1,0:T(8,128)(2,1)S(1)}, bf16[2,64,4096]{2,1,0:T(8,128)(2,1)}, u32[]{:S(2)}) copy-start(bf16[2,64,4096]{2,1,0:T(8,128)(2,1)} %all-gather.6.cloned.1.call-done) | copy-start | bytes 3145732
  534.6 1.6 copy-start.1
Sparse Core Ops, SparseCore 0:
  10.5 93.1 all-gather.9
  105.5 77.1 all-gather.7
  185.2 109.7 all-gather.11
  297.3 57.3 all-gather.5
  540.9 152.7 reduce-scatter.1
